TPU v7x, 32 devices: a whole 2x2x4 slice. The times are simulated.
32 devices in a mesh: ctx: 16 (over z, y, x), tp: 2 (over core).
Axes of the slice: x: 2, y: 2, z: 4, core: 2. Of those that a mesh axis runs over, the one named last changes fastest.
Arguments:
- query_proj: bfloat16 [2048, 1024], P('ctx', 'tp'), may hold values from -6 to 6
- key_proj: bfloat16 [2048, 1024], P('ctx', 'tp'), may hold values from -6 to 6
- value_proj: bfloat16 [2048, 1024], P('ctx', 'tp'), may hold values from -6 to 6
- out_grad: bfloat16 [2048, 1024], P('ctx', 'tp'), may hold values from -6 to 6
- short_taps: float32 [3, 3, 1024], P(None, None, 'tp'), may hold values from -3 to 3
- residues: float32 [16, 1024], P(None, 'tp'), may hold values from -1.5 to 1.5
- log_spans: float32 [16, 1024], P(None, 'tp'), as said below
- skip_gain: float32 [1024], P('tp'), may hold values from -3 to 3
Outputs:
- mixer_out: bfloat16 [2048, 1024], P('ctx', 'tp')
- grad_query: bfloat16 [2048, 1024], P('ctx', 'tp')
- grad_key: bfloat16 [2048, 1024], P('ctx', 'tp')
- grad_value: bfloat16 [2048, 1024], P('ctx', 'tp')
- grad_taps: float32 [3, 3, 1024], P(None, None, 'tp')
- grad_residues: float32 [16, 1024], P(None, 'tp')
- grad_log_spans: float32 [16, 1024], P(None, 'tp')
- grad_skip: float32 [1024], P('tp')
- grad_norm: float32 [], replicated
Inputs may be any that keep to these rules, and one draw needn't show every extreme that they name: `log_spans`: each entry lies between 3 and 4 + ln(2048).
All inputs are finite; a program needn't handle non-finite values.
Results may differ from a plain program's by a relative error of at most 0.001.
Values may be sent and summed in bfloat16 or wider, within the bound.
A program may use at most 64 MiB of HBM per device.

v0:
```python
import math

import jax
import jax.numpy as jnp
from jax import lax
from jax.sharding import PartitionSpec as P

PRECISE = lax.Precision.HIGHEST


def passed_along(value, axis, steps):
    count = lax.axis_size(axis)
    initial, last = (max(0, -steps), min(count, count - steps))
    return lax.ppermute(value, axis, [(source, source + steps) for source in range(initial, last)])


def angle_table(first, second, period, sign):
    product = first[:, None] * second[None, :] % period
    angle = product.astype(jnp.float32) * (2.0 * math.pi / period)
    return (jnp.cos(angle), sign * jnp.sin(angle))


def dense_lead(real_part, imag_part, sign):
    length = real_part.shape[0]
    index = jnp.arange(length, dtype=jnp.int32)
    cosine, sine = angle_table(index, index, length, sign)
    flat_real = real_part.reshape(length, -1)
    out_real = jnp.dot(cosine, flat_real, precision=PRECISE)
    out_imag = jnp.dot(sine, flat_real, precision=PRECISE)
    flat_imag = imag_part.reshape(length, -1)
    out_real = out_real - jnp.dot(sine, flat_imag, precision=PRECISE)
    out_imag = out_imag + jnp.dot(cosine, flat_imag, precision=PRECISE)
    return (out_real.reshape(real_part.shape), out_imag.reshape(real_part.shape))


def transform_lead(real_part, imag_part, sign):
    return dense_lead(real_part, imag_part, sign)


def forward_seq(values, count, place):
    rows, width = values.shape
    block = rows // count
    period = 2 * rows * count
    freqs = jnp.arange(2 * count, dtype=jnp.int32)
    sources = jnp.arange(count, dtype=jnp.int32)
    offsets = place * block + jnp.arange(block, dtype=jnp.int32)
    where_from = sources[None, :] * rows + offsets[:, None]
    product = freqs[None, :, None] * where_from[:, None, :] % period
    angle = product.astype(jnp.float32) * (2.0 * math.pi / period)
    joint_cos = jnp.cos(angle)
    joint_sin = -jnp.sin(angle)
    pieces = lax.all_to_all(
        values.reshape(count, block, width), "ctx", split_axis=0, concat_axis=0, tiled=True
    )
    return transform_lead(
        lax.all_to_all(
            jnp.einsum("bks,sbc->bkc", joint_cos, pieces, precision=PRECISE),
            "ctx",
            split_axis=1,
            concat_axis=0,
            tiled=True,
        ),
        lax.all_to_all(
            jnp.einsum("bks,sbc->bkc", joint_sin, pieces, precision=PRECISE),
            "ctx",
            split_axis=1,
            concat_axis=0,
            tiled=True,
        ),
        -1.0,
    )


def inverse_seq(spec_real, spec_imag, count, place):
    rows = spec_real.shape[0]
    width = spec_real.shape[2]
    back_real, back_imag = transform_lead(spec_real, spec_imag, 1.0)
    owned = 2 * place + jnp.arange(2, dtype=jnp.int32)
    turn_cos, turn_sin = angle_table(
        jnp.arange(rows, dtype=jnp.int32), owned, 2 * rows * count, 1.0
    )
    turned_real = back_real * turn_cos[:, :, None] - back_imag * turn_sin[:, :, None]
    turned_imag = back_real * turn_sin[:, :, None] + back_imag * turn_cos[:, :, None]
    section_cos, section_sin = angle_table(
        jnp.arange(count, dtype=jnp.int32), jnp.arange(2 * count, dtype=jnp.int32), 2 * count, 1.0
    )
    positions = jnp.einsum(
        "sk,bkc->sbc",
        section_cos,
        lax.all_to_all(turned_real, "ctx", split_axis=0, concat_axis=1, tiled=True),
        precision=PRECISE,
    ) - jnp.einsum(
        "sk,bkc->sbc",
        section_sin,
        lax.all_to_all(turned_imag, "ctx", split_axis=0, concat_axis=1, tiled=True),
        precision=PRECISE,
    )
    returned = lax.all_to_all(positions, "ctx", split_axis=0, concat_axis=0, tiled=True)
    return returned.reshape(rows, width) / (2.0 * rows * count)


def build_impulse(weights, rates, lags):
    return jnp.sum(weights * jnp.exp(-rates * lags), axis=0)


def mode_grads(lag_grad, residues, rates, gains, rate_grid, lags, axis):
    weighted = lag_grad[None] * jnp.exp(-rate_grid * lags[None])
    plain = jnp.sum(weighted, axis=axis + 1)
    timed = jnp.sum(weighted * lags[None], axis=axis + 1)
    return (gains * plain, residues * rates * (gains * timed - plain / (2.0 * gains)))


def body(query_proj, key_proj, value_proj, out_grad, short_taps, residues, log_spans, skip_gain):
    rows, width = query_proj.shape
    count = lax.axis_size("ctx")
    place = lax.axis_index("ctx")
    length = rows * count
    modes = residues.shape[0]
    stacked = jnp.stack((query_proj, key_proj, value_proj))
    before = passed_along(stacked[:, rows - 2 :, :], "ctx", 1)
    extended = jnp.concatenate((before, stacked), axis=1).astype(jnp.float32)
    shorted = (
        short_taps[:, 0, None, :] * extended[:, 2:, :]
        + short_taps[:, 1, None, :] * extended[:, 1 : rows + 1, :]
        + short_taps[:, 2, None, :] * extended[:, :rows, :]
    )
    mixed = shorted[1] * shorted[2]
    rates = jnp.exp(-log_spans)
    gains = jnp.sqrt(rates + 1.0 / length)
    cotangent = out_grad.astype(jnp.float32)
    inner_grad = cotangent * shorted[0]
    lags = (place * rows + jnp.arange(rows, dtype=jnp.int32)).astype(jnp.float32)[:, None]
    impulse = build_impulse((residues * gains)[:, None, :], rates[:, None, :], lags)
    mixed_real, mixed_imag = forward_seq(mixed, count, place)
    pulse_real, pulse_imag = forward_seq(impulse, count, place)
    conv = inverse_seq(
        pulse_real * mixed_real - pulse_imag * mixed_imag,
        pulse_real * mixed_imag + pulse_imag * mixed_real,
        count,
        place,
    )
    grad_real, grad_imag = forward_seq(inner_grad, count, place)
    conv_back = inverse_seq(
        pulse_real * grad_real + pulse_imag * grad_imag,
        pulse_real * grad_imag - pulse_imag * grad_real,
        count,
        place,
    )
    lag_grad = inverse_seq(
        grad_real * mixed_real + grad_imag * mixed_imag,
        grad_imag * mixed_real - grad_real * mixed_imag,
        count,
        place,
    )
    grad_res, grad_log = mode_grads(lag_grad, residues, rates, gains, rates[:, None, :], lags, 0)
    inner = conv + skip_gain[None, :] * mixed
    mixer_out = (shorted[0] * inner).astype(jnp.bfloat16)
    mixed_grad = conv_back + skip_gain[None, :] * inner_grad
    short_grad = jnp.stack((cotangent * inner, mixed_grad * shorted[2], mixed_grad * shorted[1]))
    after = passed_along(short_grad[:, :2, :], "ctx", -1)
    padded = jnp.concatenate((short_grad, after), axis=1)
    input_grads = (
        short_taps[:, 0, None, :] * padded[:, :rows, :]
        + short_taps[:, 1, None, :] * padded[:, 1 : rows + 1, :]
        + short_taps[:, 2, None, :] * padded[:, 2:, :]
    ).astype(jnp.bfloat16)
    tap_grads = jnp.stack(
        [
            jnp.sum(short_grad * extended[:, 2 - offset : 2 - offset + rows, :], axis=1)
            for offset in range(3)
        ],
        axis=1,
    )
    skip_grad = jnp.sum(inner_grad * mixed, axis=0)
    packed = jnp.concatenate(
        (tap_grads.reshape(9, width), grad_res, grad_log, skip_grad[None, :]), axis=0
    )
    totals = lax.psum(packed, "ctx")
    squares = lax.psum(jnp.sum(totals * totals), "tp")
    grad_norm = jnp.sqrt(squares)
    return (
        mixer_out,
        input_grads[0],
        input_grads[1],
        input_grads[2],
        totals[:9].reshape(3, 3, width),
        totals[9 : 9 + modes],
        totals[9 + modes : 9 + 2 * modes],
        totals[9 + 2 * modes],
        grad_norm,
    )


def solution(mesh):
    in_specs = (
        P("ctx", "tp"),
        P("ctx", "tp"),
        P("ctx", "tp"),
        P("ctx", "tp"),
        P(None, None, "tp"),
        P(None, "tp"),
        P(None, "tp"),
        P("tp"),
    )
    out_specs = (
        P("ctx", "tp"),
        P("ctx", "tp"),
        P("ctx", "tp"),
        P("ctx", "tp"),
        P(None, None, "tp"),
        P(None, "tp"),
        P(None, "tp"),
        P("tp"),
        P(),
    )
    return jax.shard_map(body, mesh=mesh, in_specs=in_specs, out_specs=out_specs, check_vma=False)
```

profile of v0, /device:TPU:0, one launch (start us, length us, event | category | flops | bytes accessed | tf_op | source)
XLA Modules:
  0.0 480.1 jit_solution(18260819579810384376)
XLA Ops:
  7.9 4.8 %collective-permute-start = (bf16[3,2,512]{2,1,0:T(2,128)(2,1)S(1)}, bf16[3,2,512]{2,1,0:T(2,128)(2,1)S(1)}, u32[]{:S(2)}, u32[]{:S(2)}) collective-permute-start(bf16[3,2,512]{2,1,0:T(2,128)(2,1)S(1)} %pad_maximum_fusion.4), channel_id=1, source_target_pairs={{0,2},{2,4},{4,6},{6,8},{8,10},{10,12},{12,14},{14,16},{16,18},{18... | collective-permute-start | bytes 18440 | tf_op jit(solution)/shard_map/ppermute | solution.py:14
  16.2 7.7 %all-to-all-start.3 = ((f32[16,8,512]{2,1,0:T(8,128)}), f32[16,8,512]{2,1,0:T(8,128)S(1)}, u32[]{:S(2)}, u32[]{:S(2)}) async-start(f32[16,8,512]{2,1,0:T(8,128)} %multiply_bitcast_fusion.1), calls=%async_computation.3 | async-start | bytes 524288 | tf_op jit(solution)/shard_map/all_to_all | solution.py:52
  24.7 7.7 %all-to-all-done.3 = f32[16,8,512]{2,1,0:T(8,128)S(1)} async-done(((f32[16,8,512]{2,1,0:T(8,128)}), f32[16,8,512]{2,1,0:T(8,128)S(1)}, u32[]{:S(2)}, u32[]{:S(2)}) %all-to-all-start.3) | async-done | bytes 262176 | tf_op jit(solution)/shard_map/all_to_all | solution.py:52
  32.4 3.8 all-to-all-start.9
  38.4 6.8 %all-to-all-done.9 = f32[16,8,512]{2,1,0:T(8,128)S(1)} async-done(((f32[16,8,512]{2,1,0:T(8,128)}), f32[16,8,512]{2,1,0:T(8,128)S(1)}, u32[]{:S(2)}, u32[]{:S(2)}) %all-to-all-start.9) | async-done | bytes 262176 | tf_op jit(solution)/shard_map/all_to_all | solution.py:52
  45.2 3.6 all-to-all-start.5
  50.9 12.2 %all-to-all-done.5 = f32[8,32,512]{2,0,1:T(8,128)S(1)} async-done(((f32[8,32,512]{2,0,1:T(8,128)}), f32[8,32,512]{2,0,1:T(8,128)S(1)}, u32[]{:S(2)}, u32[]{:S(2)}) %all-to-all-start.5) | async-done | bytes 524320 | tf_op jit(solution)/shard_map/all_to_all | solution.py:63
  63.1 3.8 all-to-all-start.4
  69.0 12.1 %all-to-all-done.4 = f32[8,32,512]{2,0,1:T(8,128)S(1)} async-done(((f32[8,32,512]{2,0,1:T(8,128)}), f32[8,32,512]{2,0,1:T(8,128)S(1)}, u32[]{:S(2)}, u32[]{:S(2)}) %all-to-all-start.4) | async-done | bytes 524320 | tf_op jit(solution)/shard_map/all_to_all | solution.py:56
  81.2 4.2 all-to-all-start.10
  92.0 7.3 %all-to-all-done.10 = f32[8,32,512]{2,0,1:T(8,128)} async-done(((f32[8,32,512]{2,0,1:T(8,128)}), f32[8,32,512]{2,0,1:T(8,128)}, u32[]{:S(2)}, u32[]{:S(2)}) %all-to-all-start.10) | async-done | bytes 524320 | tf_op jit(solution)/shard_map/all_to_all | solution.py:56
  99.3 4.5 all-to-all-start.11
  110.6 6.8 %all-to-all-done.11 = f32[8,32,512]{2,0,1:T(8,128)} async-done(((f32[8,32,512]{2,0,1:T(8,128)}), f32[8,32,512]{2,0,1:T(8,128)}, u32[]{:S(2)}, u32[]{:S(2)}) %all-to-all-start.11) | async-done | bytes 524320 | tf_op jit(solution)/shard_map/all_to_all | solution.py:63
  132.1 17.5 %all_to_all.228 = f32[128,2,512]{2,1,0:T(2,128)} all-to-all(f32[128,2,512]{2,1,0:T(2,128)S(1)} %get-tuple-element.29), channel_id=1, replica_groups=mesh['ctx'=16,'tp'=2] {'ctx'}, dimensions={0} | all-to-all | bytes 1048576 | tf_op jit(solution)/shard_map/all_to_all | solution.py:95
  149.6 4.4 all-to-all-start.15
  158.1 9.6 %all-to-all-done.15 = f32[128,2,512]{2,1,0:T(2,128)S(1)} async-done(((f32[128,2,512]{2,1,0:T(2,128)}), f32[128,2,512]{2,1,0:T(2,128)S(1)}, u32[]{:S(2)}, u32[]{:S(2)}) %all-to-all-start.15) | async-done | bytes 524320 | tf_op jit(solution)/shard_map/all_to_all | solution.py:90
  173.6 3.8 all-to-all-start.17
  178.1 7.8 %all-to-all-done.17 = f32[16,8,512]{2,1,0:T(8,128)S(1)} async-done(((f32[16,8,512]{2,1,0:T(8,128)}), f32[16,8,512]{2,1,0:T(8,128)S(1)}, u32[]{:S(2)}, u32[]{:S(2)}) %all-to-all-start.17) | async-done | bytes 262176 | tf_op jit(solution)/shard_map/all_to_all | solution.py:98
  188.8 11.8 %all_to_all.229 = f32[16,8,512]{2,1,0:T(8,128)S(1)} all-to-all(f32[16,8,512]{2,1,0:T(8,128)S(1)} %bitcast.223), channel_id=1, replica_groups=mesh['ctx'=16,'tp'=2] {'ctx'}, dimensions={0} | all-to-all | bytes 524288 | tf_op jit(solution)/shard_map/all_to_all | solution.py:52
  202.7 3.6 all-to-all-start.1
  208.4 9.8 %all-to-all-done.1 = f32[8,32,512]{2,0,1:T(8,128)S(1)} async-done(((f32[8,32,512]{2,0,1:T(8,128)}), f32[8,32,512]{2,0,1:T(8,128)S(1)}, u32[]{:S(2)}, u32[]{:S(2)}) %all-to-all-start.1) | async-done | bytes 524320 | tf_op jit(solution)/shard_map/all_to_all | solution.py:56
  218.2 4.4 all-to-all-start.2
  225.7 9.9 %all-to-all-done.2 = f32[8,32,512]{2,0,1:T(8,128)} async-done(((f32[8,32,512]{2,0,1:T(8,128)}), f32[8,32,512]{2,0,1:T(8,128)}, u32[]{:S(2)}, u32[]{:S(2)}) %all-to-all-start.2) | async-done | bytes 524320 | tf_op jit(solution)/shard_map/all_to_all | solution.py:63
  260.3 17.6 %all_to_all.230 = f32[128,2,512]{2,1,0:T(2,128)} all-to-all(f32[128,2,512]{2,1,0:T(2,128)S(1)} %get-tuple-element.25), channel_id=1, replica_groups=mesh['ctx'=16,'tp'=2] {'ctx'}, dimensions={0} | all-to-all | bytes 1048576 | tf_op jit(solution)/shard_map/all_to_all | solution.py:95
  277.9 17.3 %all_to_all.231 = f32[128,2,512]{2,1,0:T(2,128)S(1)} all-to-all(f32[128,2,512]{2,1,0:T(2,128)S(1)} %get-tuple-element.26), channel_id=1, replica_groups=mesh['ctx'=16,'tp'=2] {'ctx'}, dimensions={0} | all-to-all | bytes 1048576 | tf_op jit(solution)/shard_map/all_to_all | solution.py:90
  295.2 17.3 %all_to_all.232 = f32[128,2,512]{2,1,0:T(2,128)S(1)} all-to-all(f32[128,2,512]{2,1,0:T(2,128)S(1)} %get-tuple-element.40), channel_id=1, replica_groups=mesh['ctx'=16,'tp'=2] {'ctx'}, dimensions={0} | all-to-all | bytes 1048576 | tf_op jit(solution)/shard_map/all_to_all | solution.py:90
  312.5 3.8 all-to-all-start.7
  330.1 3.8 all-to-all-start.14
  335.5 7.0 %all-to-all-done.14 = f32[16,8,512]{2,1,0:T(8,128)S(1)} async-done(((f32[16,8,512]{2,1,0:T(8,128)}), f32[16,8,512]{2,1,0:T(8,128)S(1)}, u32[]{:S(2)}, u32[]{:S(2)}) %all-to-all-start.14) | async-done | bytes 262176 | tf_op jit(solution)/shard_map/all_to_all | solution.py:98
  342.5 11.8 %all_to_all.233 = f32[16,8,512]{2,1,0:T(8,128)S(1)} all-to-all(f32[16,8,512]{2,1,0:T(8,128)S(1)} %copy.111), channel_id=1, replica_groups=mesh['ctx'=16,'tp'=2] {'ctx'}, dimensions={0} | all-to-all | bytes 524288 | tf_op jit(solution)/shard_map/all_to_all | solution.py:98
  355.9 4.2 collective-permute-done.1
  362.3 101.6 %all-reduce.2.cloned.1.call-done = f32[42,512]{1,0:T(8,128)} async-done(((f32[42,512]{1,0:T(8,128)}), f32[42,512]{1,0:T(8,128)}) %all-reduce.2.cloned.1.call-update) | async-done | bytes 86032 | tf_op jit(solution)/shard_map/psum | solution.py:178
  (170 shorter events, 110.4 us)
Async XLA Ops:
  7.9 6.2 %collective-permute-start = (bf16[3,2,512]{2,1,0:T(2,128)(2,1)S(1)}, bf16[3,2,512]{2,1,0:T(2,128)(2,1)S(1)}, u32[]{:S(2)}, u32[]{:S(2)}) collective-permute-start(bf16[3,2,512]{2,1,0:T(2,128)(2,1)S(1)} %pad_maximum_fusion.4), channel_id=1, source_target_pairs={{0,2},{2,4},{4,6},{6,8},{8,10},{10,12},{12,14},{14,16},{16,18},{18... | collective-permute-start | bytes 18440 | tf_op jit(solution)/shard_map/ppermute | solution.py:14
  15.5 8.4 %copy-start.14 = (bf16[128,512]{1,0:T(8,128)(2,1)S(1)}, bf16[128,512]{1,0:T(8,128)(2,1)}, u32[]{:S(2)}) copy-start(bf16[128,512]{1,0:T(8,128)(2,1)} %param.11) | copy-start | bytes 393220
  16.2 16.2 %all-to-all-start.3 = ((f32[16,8,512]{2,1,0:T(8,128)}), f32[16,8,512]{2,1,0:T(8,128)S(1)}, u32[]{:S(2)}, u32[]{:S(2)}) async-start(f32[16,8,512]{2,1,0:T(8,128)} %multiply_bitcast_fusion.1), calls=%async_computation.3 | async-start | bytes 524288 | tf_op jit(solution)/shard_map/all_to_all | solution.py:52
  32.4 12.8 %all-to-all-start.9 = ((f32[16,8,512]{2,1,0:T(8,128)}), f32[16,8,512]{2,1,0:T(8,128)S(1)}, u32[]{:S(2)}, u32[]{:S(2)}) async-start(f32[16,8,512]{2,1,0:T(8,128)} %fusion.270), calls=%async_computation.9 | async-start | bytes 524288 | tf_op jit(solution)/shard_map/all_to_all | solution.py:52
  45.2 17.9 %all-to-all-start.5 = ((f32[8,32,512]{2,0,1:T(8,128)}), f32[8,32,512]{2,0,1:T(8,128)S(1)}, u32[]{:S(2)}, u32[]{:S(2)}) async-start(f32[8,32,512]{2,0,1:T(8,128)} %copy.105), calls=%async_computation.5 | async-start | bytes 1048576 | tf_op jit(solution)/shard_map/all_to_all | solution.py:63
  63.1 18.1 %all-to-all-start.4 = ((f32[8,32,512]{2,0,1:T(8,128)}), f32[8,32,512]{2,0,1:T(8,128)S(1)}, u32[]{:S(2)}, u32[]{:S(2)}) async-start(f32[8,32,512]{2,0,1:T(8,128)} %copy.102), calls=%async_computation.4 | async-start | bytes 1048576 | tf_op jit(solution)/shard_map/all_to_all | solution.py:56
  81.2 5.6 %copy-start.5 = (f32[8,32,512]{2,0,1:T(8,128)}, f32[8,32,512]{2,0,1:T(8,128)S(1)}, u32[]{:S(2)}) copy-start(f32[8,32,512]{2,0,1:T(8,128)S(1)} %all-to-all-done.4) | copy-start | bytes 1572868
  81.2 18.1 %all-to-all-start.10 = ((f32[8,32,512]{2,0,1:T(8,128)}), f32[8,32,512]{2,0,1:T(8,128)}, u32[]{:S(2)}, u32[]{:S(2)}) async-start(f32[8,32,512]{2,0,1:T(8,128)} %copy.113), calls=%async_computation.10 | async-start | bytes 1048576 | tf_op jit(solution)/shard_map/all_to_all | solution.py:56
  85.8 43.7 %copy-start.12 = (f32[128,2]{1,0:T(8,128)}, f32[128,2]{1,0:T(8,128)S(1)}, u32[]{:S(2)}) copy-start(f32[128,2]{1,0:T(8,128)S(1)} %copy.108) | copy-start | bytes 3076
  99.3 18.1 %all-to-all-start.11 = ((f32[8,32,512]{2,0,1:T(8,128)}), f32[8,32,512]{2,0,1:T(8,128)}, u32[]{:S(2)}, u32[]{:S(2)}) async-start(f32[8,32,512]{2,0,1:T(8,128)} %copy.116), calls=%async_computation.11 | async-start | bytes 1048576 | tf_op jit(solution)/shard_map/all_to_all | solution.py:63
  117.4 1.6 copy-start.3
  120.0 1.8 copy-start
  149.6 18.1 %all-to-all-start.15 = ((f32[128,2,512]{2,1,0:T(2,128)}), f32[128,2,512]{2,1,0:T(2,128)S(1)}, u32[]{:S(2)}, u32[]{:S(2)}) async-start(f32[128,2,512]{2,1,0:T(2,128)} %get-tuple-element.30), calls=%async_computation.15 | async-start | bytes 1048576 | tf_op jit(solution)/shard_map/all_to_all | solution.py:90
  168.5 3.7 copy-start.7
  172.3 5.2 %copy-start.17 = (f32[16,512]{1,0:T(8,128)S(1)}, f32[16,512]{1,0:T(8,128)}, u32[]{:S(2)}) copy-start(f32[16,512]{1,0:T(8,128)} %param.13) | copy-start | bytes 98308
  172.3 5.2 %copy-start.19 = (f32[16,512]{1,0:T(8,128)S(1)}, f32[16,512]{1,0:T(8,128)}, u32[]{:S(2)}) copy-start(f32[16,512]{1,0:T(8,128)} %param.14) | copy-start | bytes 98308
  173.6 12.4 %all-to-all-start.17 = ((f32[16,8,512]{2,1,0:T(8,128)}), f32[16,8,512]{2,1,0:T(8,128)S(1)}, u32[]{:S(2)}, u32[]{:S(2)}) async-start(f32[16,8,512]{2,1,0:T(8,128)} %copy.123), calls=%async_computation.17 | async-start | bytes 524288 | tf_op jit(solution)/shard_map/all_to_all | solution.py:98
  202.7 15.5 %all-to-all-start.1 = ((f32[8,32,512]{2,0,1:T(8,128)}), f32[8,32,512]{2,0,1:T(8,128)S(1)}, u32[]{:S(2)}, u32[]{:S(2)}) async-start(f32[8,32,512]{2,0,1:T(8,128)} %copy.96), calls=%async_computation.1 | async-start | bytes 1048576 | tf_op jit(solution)/shard_map/all_to_all | solution.py:56
  218.2 17.3 %all-to-all-start.2 = ((f32[8,32,512]{2,0,1:T(8,128)}), f32[8,32,512]{2,0,1:T(8,128)}, u32[]{:S(2)}, u32[]{:S(2)}) async-start(f32[8,32,512]{2,0,1:T(8,128)} %copy.99), calls=%async_computation.2 | async-start | bytes 1048576 | tf_op jit(solution)/shard_map/all_to_all | solution.py:63
  249.1 2.8 copy-start.4
  253.5 4.0 copy-start.13
  312.5 17.6 %all-to-all-start.7 = ((f32[128,2,512]{2,1,0:T(2,128)}), f32[128,2,512]{2,1,0:T(2,128)S(1)}, u32[]{:S(2)}, u32[]{:S(2)}) async-start(f32[128,2,512]{2,1,0:T(2,128)} %get-tuple-element.41), calls=%async_computation.7 | async-start | bytes 1048576 | tf_op jit(solution)/shard_map/all_to_all | solution.py:95
  321.3 3.7 copy-start.8
  330.1 12.4 %all-to-all-start.14 = ((f32[16,8,512]{2,1,0:T(8,128)}), f32[16,8,512]{2,1,0:T(8,128)S(1)}, u32[]{:S(2)}, u32[]{:S(2)}) async-start(f32[16,8,512]{2,1,0:T(8,128)} %copy.120), calls=%async_computation.14 | async-start | bytes 524288 | tf_op jit(solution)/shard_map/all_to_all | solution.py:98
  334.0 129.9 %all-reduce.2.cloned.1.call-start = ((), (), s32[]{:S(2)}) async-start(), calls=%async_computation.18 | async-start | bytes 196608 | tf_op jit(solution)/shard_map/psum | solution.py:178
  334.8 19.4 %copy-start.15 = (bf16[128,512]{1,0:T(8,128)(2,1)S(1)}, bf16[128,512]{1,0:T(8,128)(2,1)}, u32[]{:S(2)}) copy-start(bf16[128,512]{1,0:T(8,128)(2,1)} %param.11) | copy-start | bytes 393220
  334.9 19.4 %copy-start.23 = (f32[512]{0:T(512)S(1)}, f32[512]{0:T(512)}, u32[]{:S(2)}) copy-start(f32[512]{0:T(512)} %param.15) | copy-start | bytes 6148
  354.4 1.4 copy-start.18
  354.4 1.4 copy-start.20
  354.6 5.6 %collective-permute-start.1 = (f32[3,2,512]{2,1,0:T(2,128)S(1)}, f32[3,2,512]{2,1,0:T(2,128)S(1)}, u32[]{:S(2)}, u32[]{:S(2)}) collective-permute-start(f32[3,2,512]{2,1,0:T(2,128)S(1)} %slice.95), channel_id=1, source_target_pairs={{2,0},{4,2},{6,4},{8,6},{10,8},{12,10},{14,12},{16,14},{18,16},{20... | collective-permute-start | bytes 36872 | tf_op jit(solution)/shard_map/ppermute | solution.py:14
  463.9 6.2 %slice-start = ((f32[42,512]{1,0:T(8,128)}), f32[9,512]{1,0:T(8,128)S(1)}, s32[]{:S(2)}) async-start(f32[42,512]{1,0:T(8,128)} %all-reduce.2.cloned.1.call-done), calls=%async_computation.19 | async-start | bytes 65536 | tf_op jit(solution)/shard_map/slice | solution.py:186
  463.9 6.8 %copy-start.16 = (f32[42,512]{1,0:T(8,128)S(1)}, f32[42,512]{1,0:T(8,128)}, u32[]{:S(2)}) copy-start(f32[42,512]{1,0:T(8,128)} %all-reduce.2.cloned.1.call-done) | copy-start | bytes 258052
  (8 other events, 9.5 us)
Sparse Core Ops, SparseCore 0:
  361.7 102.1 all-reduce.1
where the time goes:
time: 490 us; the launch traced here: 480 us
  waiting for transfers between devices  207 us (42%)
  blocking collectives  96.5 us (20%)
  starting transfers between devices  57.7 us (12%)
  local copies, waits for them, and re-layouts  44.5 us (9%)
  matrix products  41.3 us (8%)
  between operations  16.9 us (3%)
  other arithmetic  16.5 us (3%)
    psum x1, waiting for transfers between devices, body(): totals = lax.psum(packed, 'ctx')  102 us
    all_to_all x2, blocking collectives, inverse_seq(): lax.all_to_all(turned_imag, 'ctx', split_axis=0, concat_axis=1, tiled=True)  35.1 us
    all_to_all x2, blocking collectives, inverse_seq(): lax.all_to_all(turned_real, 'ctx', split_axis=0, concat_axis=1, tiled=True)  34.7 us
    all_to_all x3, waiting for transfers between devices, forward_seq(): lax.all_to_all(jnp.einsum('bks,sbc->bkc', joint_cos, pieces, precision=PR...  29.3 us
    all_to_all x3, waiting for transfers between devices, forward_seq(): lax.all_to_all(jnp.einsum('bks,sbc->bkc', joint_sin, pieces, precision=PR...  28.9 us
    all_to_all x2, waiting for transfers between devices, inverse_seq(): lax.all_to_all(positions, 'ctx', split_axis=0, concat_axis=0, tiled=True)  14.8 us
    all_to_all x2, waiting for transfers between devices, forward_seq(): lax.all_to_all(values.reshape(count, block, width), 'ctx', split_axis=0,...  14.5 us
    all_to_all x3, starting transfers between devices, forward_seq(): lax.all_to_all(jnp.einsum('bks,sbc->bkc', joint_sin, pieces, precision=PR...  12.5 us
  transfers between devices with their start and end apart: 15, of which 15 were waited for; matrix products, arithmetic and copies ran while one was open for 7% of the time, Pallas kernels for 0%

commit v1 on v0

v1 whole, which is shorter than its diff:
```python
import functools

import jax
import jax.numpy as jnp
from jax import lax
from jax.experimental import pallas as pl
from jax.experimental.pallas import tpu as pltpu
from jax.sharding import PartitionSpec as P

MESH = pl.DeviceIdType.MESH
UNROLL = 8


def radices_of(count):
    out = []
    while count > 1:
        radix = 4 if count % 4 == 0 else 2
        out.append(radix)
        count //= radix
    return tuple(out)


def kernel(
    count, tps, radices, per,
    q_ref, k_ref, v_ref, og_ref, taps_ref, res_ref, span_ref, skip_ref,
    mix_ref, gq_ref, gk_ref, gv_ref, gtaps_ref, gres_ref, glog_ref, gskip_ref, norm_ref,
    halo_out, halo_in, xe, og, sh, mx, ig, sg, hs, es, yp, zp,
    tot_out, tot_in, parts, parts_in, whole, norm_out, norm_in,
    halo_ss, halo_rs, tot_ss, tot_rs, part_ss, part_rs, whole_ss, whole_rs, norm_ss, norm_rs,
):
    me = lax.axis_index("ctx")
    core = lax.axis_index("tp")
    rows, width = q_ref.shape
    modes = res_ref.shape[0]
    length = rows * count
    lanes = width // 128
    ins = (q_ref, k_ref, v_ref)

    def at(peer):
        return {"ctx": peer, "tp": core}

    barrier = pltpu.get_barrier_semaphore()

    def greet(i, carry):
        pl.semaphore_signal(barrier, inc=1, device_id=at(lax.rem(me + i, count)), device_id_type=MESH)
        return carry

    lax.fori_loop(1, count, greet, 0)

    def greet_core(i, carry):
        pl.semaphore_signal(
            barrier, inc=1, device_id={"ctx": me, "tp": lax.rem(core + i, tps)}, device_id_type=MESH
        )
        return carry

    lax.fori_loop(1, tps, greet_core, 0)

    for w in range(3):
        xe[w, 0:8, :] = jnp.zeros((8, width), jnp.float32)
        xe[w, 8 : 8 + rows, :] = ins[w][...].astype(jnp.float32)
    og[0:rows, :] = og_ref[...].astype(jnp.float32)
    for w in range(3):
        halo_out[0, 2 * w : 2 * w + 2, :] = xe[w, 8 + rows - 2 : 8 + rows, :]
        halo_out[1, 2 * w : 2 * w + 2, :] = xe[w, 8:10, :]
    halo_out[0, 6:8, :] = jnp.zeros((2, width), jnp.float32)
    halo_out[1, 6:8, :] = og[0:2, :]

    pl.semaphore_wait(barrier, count - 1 + tps - 1)

    def halo_copy(side):
        peer = lax.rem(me + (1 if side == 0 else count - 1), count)
        return pltpu.make_async_remote_copy(
            src_ref=halo_out.at[side], dst_ref=halo_in.at[side],
            send_sem=halo_ss.at[side], recv_sem=halo_rs.at[side],
            device_id=at(peer), device_id_type=MESH,
        )

    for side in range(2):
        halo_copy(side).start()

    def short_rows(low, size):
        for w in range(3):
            sh[w, low : low + size, :] = (
                taps_ref[w, 0:1, :] * xe[w, 8 + low : 8 + low + size, :]
                + taps_ref[w, 1:2, :] * xe[w, 7 + low : 7 + low + size, :]
                + taps_ref[w, 2:3, :] * xe[w, 6 + low : 6 + low + size, :]
            )
        mx[low : low + size, :] = sh[1, low : low + size, :] * sh[2, low : low + size, :]
        ig[low : low + size, :] = og[low : low + size, :] * sh[0, low : low + size, :]

    short_rows(8, rows - 8)
    rates = jnp.exp(-span_ref[...])
    gains = jnp.sqrt(rates + 1.0 / length)
    weights = res_ref[...] * gains
    decay = jnp.exp(-rates)

    for side in range(2):
        halo_copy(side).wait()
    is_first = me == 0
    is_last = me == count - 1
    for w in range(3):
        xe[w, 6:8, :] = jnp.where(is_first, 0.0, halo_in[0, 2 * w : 2 * w + 2, :])
        xe[w, 8 + rows : 16 + rows, :] = jnp.zeros((8, width), jnp.float32)
        xe[w, 8 + rows : 10 + rows, :] = halo_in[1, 2 * w : 2 * w + 2, :]
    og[rows : rows + 8, :] = jnp.zeros((8, width), jnp.float32)
    og[rows : rows + 2, :] = halo_in[1, 6:8, :]
    short_rows(0, 8)
    short_rows(rows, 8)

    steps = rows // UNROLL
    zero = jnp.zeros((modes, width), jnp.float32)

    def end_states(n, carry):
        h, b = carry
        low = pl.multiple_of(n * UNROLL, UNROLL)
        high = pl.multiple_of((steps - 1 - n) * UNROLL, UNROLL)
        x = mx[pl.ds(low, UNROLL), :]
        g = ig[pl.ds(high, UNROLL), :]
        for i in range(UNROLL):
            h = decay * h + x[i : i + 1, :]
            b = decay * b + g[UNROLL - 1 - i : UNROLL - i, :]
        return h, b

    end_h, end_b = lax.fori_loop(0, steps, end_states, (zero, zero))

    def spread(chunks):
        return jnp.exp(-rates * (jnp.float32(rows) * chunks.astype(jnp.float32)))

    def fixed_spread(chunks):
        return jnp.exp(-rates * float(rows * chunks))

    last = len(radices) - 1

    def tot_copy(stage, stride, radix, off):
        digit = lax.rem(me // stride, radix)
        other = lax.rem(digit + off, radix)
        peer = me + (other - digit) * stride
        if stage == last:
            which = jnp.where(other > digit, 0, 1)
            source = tot_out.at[stage, which]
            target = tot_in.at[stage, off - 1, 0]
        else:
            source = tot_out.at[stage]
            target = tot_in.at[stage, off - 1]
        return pltpu.make_async_remote_copy(
            src_ref=source, dst_ref=target,
            send_sem=tot_ss.at[stage, off - 1], recv_sem=tot_rs.at[stage, off - 1],
            device_id=at(peer), device_id_type=MESH,
        )

    def forward(n, carry):
        h, p, e = carry
        low = pl.multiple_of(n * UNROLL, UNROLL)
        x = mx[pl.ds(low, UNROLL), :]
        for i in range(UNROLL):
            h = decay * h + x[i : i + 1, :]
            p = decay * p + h
            e = e * decay
            hs[low + i] = h
            es[low + i] = e
            y = weights * h
            y = y[0:8] + y[8:16]
            for c in range(lanes):
                yp[c, pl.ds(pl.multiple_of((low + i) * 8, 8), 8), :] = y[:, c * 128 : c * 128 + 128]
        return h, p, e

    def backward(n, carry):
        b, q, plain, timed = carry
        low = pl.multiple_of((steps - 1 - n) * UNROLL, UNROLL)
        g = ig[pl.ds(low, UNROLL), :]
        for i in range(UNROLL - 1, -1, -1):
            row = g[i : i + 1, :]
            h = hs[low + i]
            ab = decay * b
            timed = timed + ab * h
            plain = plain + row * h
            q = decay * q + ab
            b = ab + row
            z = weights * b
            z = z[0:8] + z[8:16]
            for c in range(lanes):
                zp[c, pl.ds(pl.multiple_of((low + i) * 8, 8), 8), :] = z[:, c * 128 : c * 128 + 128]
        return b, q, plain, timed

    own_h, own_b = end_h, end_b
    carry_h, carry_b = zero, zero
    stride = 1
    for stage, radix in enumerate(radices):
        tot_out[stage, 0] = own_h
        tot_out[stage, 1] = own_b
        for off in range(1, radix):
            tot_copy(stage, stride, radix, off).start()
        if stage == 0:
            _, sum_h, _ = lax.fori_loop(0, steps, forward, (zero, zero, zero + 1.0))
        if stage == last:
            _, sum_b, plain, timed = lax.fori_loop(0, steps, backward, (zero, zero, zero, zero))
        digit = lax.rem(me // stride, radix)
        inside = lax.rem(me, stride)
        if stage != last:
            new_h = own_h * spread(stride * (radix - 1 - digit))
            new_b = own_b * spread(stride * digit)
        for off in range(1, radix):
            tot_copy(stage, stride, radix, off).wait()
            other = lax.rem(digit - off + radix, radix)
            lower = other < digit
            chunks = jnp.where(
                lower, inside + stride * (digit - 1 - other),
                stride - 1 - inside + stride * (other - digit - 1),
            )
            far = spread(chunks)
            got_h = tot_in[stage, off - 1, 0]
            got_b = got_h if stage == last else tot_in[stage, off - 1, 1]
            carry_h = carry_h + jnp.where(lower, far * got_h, 0.0)
            carry_b = carry_b + jnp.where(lower, 0.0, far * got_b)
            if stage != last:
                new_h = new_h + got_h * spread(stride * (radix - 1 - other))
                new_b = new_b + got_b * spread(stride * other)
        if stage != last:
            own_h, own_b = new_h, new_b
        stride *= radix

    across = fixed_spread(1)
    plain = plain + decay * carry_h * end_b
    timed = (
        timed + decay * carry_h * sum_b + decay * carry_b * sum_h
        + float(rows) * across * decay * carry_h * carry_b
    )
    part_res = gains * plain
    part_log = res_ref[...] * rates * (gains * timed - plain / (2.0 * gains))
    weight_h = weights * carry_h
    weight_b = weights * carry_b

    def correct(n, carry):
        low = n * UNROLL
        for i in range(UNROLL):
            e = es[low + i]
            y = weight_h * e
            z = weight_b * e
            y = y[0:8] + y[8:16]
            z = z[0:8] + z[8:16]
            here = pl.ds(pl.multiple_of((low + i) * 8, 8), 8)
            there = pl.ds(pl.multiple_of((rows - 1 - low - i) * 8, 8), 8)
            for c in range(lanes):
                yp[c, here, :] += y[:, c * 128 : c * 128 + 128]
                zp[c, there, :] += z[:, c * 128 : c * 128 + 128]
        return carry

    lax.fori_loop(0, steps, correct, 0)

    h_next = decay * (end_h + across * carry_h) + mx[rows : rows + 1, :]
    h_after = decay * h_next + mx[rows + 1 : rows + 2, :]
    b_after = (carry_b - ig[rows : rows + 1, :]) * jnp.exp(rates)
    y_next = jnp.concatenate(
        (jnp.sum(weights * h_next, axis=0, keepdims=True), jnp.sum(weights * h_after, axis=0, keepdims=True)), axis=0
    )
    z_next = jnp.concatenate(
        (jnp.sum(weights * carry_b, axis=0, keepdims=True), jnp.sum(weights * b_after, axis=0, keepdims=True)), axis=0
    )
    two = slice(rows, rows + 2)
    y_next = y_next + skip_ref[...] * mx[two, :]
    z_next = z_next + skip_ref[...] * ig[two, :]
    sg[0, two, :] = jnp.where(is_last, 0.0, og[two, :] * y_next)
    sg[1, two, :] = jnp.where(is_last, 0.0, z_next * sh[2, two, :])
    sg[2, two, :] = jnp.where(is_last, 0.0, z_next * sh[1, two, :])

    def put(row, c, value):
        parts[(row // 8) * lanes + c, row % 8 : row % 8 + value.shape[0], :] = value

    outs = (gq_ref, gk_ref, gv_ref)
    for c in range(lanes):
        cols = slice(c * 128, c * 128 + 128)
        for low in range(0, modes, 8):
            put(low, c, part_res[low : low + 8, cols])
            put(modes + low, c, part_log[low : low + 8, cols])
        y = yp[c, pl.ds(0, rows, stride=8), :]
        z = zp[c, pl.ds(0, rows, stride=8), :]
        for i in range(1, 8):
            y = y + yp[c, pl.ds(i, rows, stride=8), :]
            z = z + zp[c, pl.ds(i, rows, stride=8), :]
        mixed = mx[0:rows, cols]
        inner_grad = ig[0:rows, cols]
        inner = y + skip_ref[:, cols] * mixed
        mixed_grad = z + skip_ref[:, cols] * inner_grad
        mix_ref[:, cols] = (sh[0, 0:rows, cols] * inner).astype(jnp.bfloat16)
        sg[0, 0:rows, cols] = og[0:rows, cols] * inner
        sg[1, 0:rows, cols] = mixed_grad * sh[2, 0:rows, cols]
        sg[2, 0:rows, cols] = mixed_grad * sh[1, 0:rows, cols]
        for w in range(3):
            for j in range(3):
                put(
                    2 * modes + 3 * w + j, c,
                    jnp.sum(sg[w, 0:rows, cols] * xe[w, 8 - j : 8 - j + rows, cols], axis=0, keepdims=True),
                )
        put(2 * modes + 9, c, jnp.sum(inner_grad * mixed, axis=0, keepdims=True))
        put(2 * modes + 10, c, jnp.zeros((6, 128), jnp.float32))
    used = (2 * modes + 16) // 8 * lanes
    for n in range(used, count * per):
        parts[n] = jnp.zeros((8, 128), jnp.float32)

    def part_copy(i):
        peer = lax.rem(me + i, count)
        return pltpu.make_async_remote_copy(
            src_ref=parts.at[pl.ds(peer * per, per)], dst_ref=parts_in.at[me],
            send_sem=part_ss.at[i], recv_sem=part_rs.at[i], device_id=at(peer), device_id_type=MESH,
        )

    def whole_copy(i):
        peer = lax.rem(me + i, count)
        mine = whole.at[pl.ds(me * per, per)]
        return pltpu.make_async_remote_copy(
            src_ref=mine, dst_ref=mine,
            send_sem=whole_ss.at[i], recv_sem=whole_rs.at[i], device_id=at(peer), device_id_type=MESH,
        )

    def norm_copy(i):
        peer = lax.rem(core + i, tps)
        return pltpu.make_async_remote_copy(
            src_ref=norm_out, dst_ref=norm_in.at[core],
            send_sem=norm_ss.at[i], recv_sem=norm_rs.at[i],
            device_id={"ctx": me, "tp": peer}, device_id_type=MESH,
        )

    def start_all(make, n):
        def one(i, carry):
            make(i).start()
            return carry

        lax.fori_loop(1, n, one, 0)

    def wait_all(make, n):
        def one(i, carry):
            make(i).wait()
            return carry

        lax.fori_loop(1, n, one, 0)

    start_all(part_copy, count)
    for c in range(lanes):
        cols = slice(c * 128, c * 128 + 128)
        for w in range(3):
            outs[w][:, cols] = (
                taps_ref[w, 0:1, cols] * sg[w, 0:rows, cols]
                + taps_ref[w, 1:2, cols] * sg[w, 1 : rows + 1, cols]
                + taps_ref[w, 2:3, cols] * sg[w, 2 : rows + 2, cols]
            ).astype(jnp.bfloat16)
    parts_in[me] = parts[pl.ds(me * per, per)]
    wait_all(part_copy, count)

    total = parts_in[0]
    for n in range(1, count):
        total = total + parts_in[n]
    whole[pl.ds(me * per, per)] = total
    start_all(whole_copy, count)
    wait_all(whole_copy, count)

    squares = jnp.zeros((8, 128), jnp.float32)
    for n in range(used):
        squares = squares + whole[n] * whole[n]
    norm_out[...] = squares
    start_all(norm_copy, tps)
    norm_in[core] = squares
    for c in range(lanes):
        cols = slice(c * 128, c * 128 + 128)
        for low in range(0, modes, 8):
            gres_ref[low : low + 8, cols] = whole[(low // 8) * lanes + c]
            glog_ref[low : low + 8, cols] = whole[((modes + low) // 8) * lanes + c]
        for n in range(9):
            row = 2 * modes + n
            gtaps_ref[n // 3, n % 3 : n % 3 + 1, cols] = whole[(row // 8) * lanes + c, row % 8 : row % 8 + 1, :]
        row = 2 * modes + 9
        gskip_ref[:, cols] = whole[(row // 8) * lanes + c, row % 8 : row % 8 + 1, :]
    wait_all(norm_copy, tps)
    squares = norm_in[0]
    for n in range(1, tps):
        squares = squares + norm_in[n]
    norm_ref[...] = jnp.broadcast_to(jnp.sqrt(jnp.sum(squares, keepdims=True)), (8, 128))


def body(query_proj, key_proj, value_proj, out_grad, short_taps, residues, log_spans, skip_gain):
    rows, width = query_proj.shape
    count = lax.axis_size("ctx")
    tps = lax.axis_size("tp")
    modes = residues.shape[0]
    lanes = width // 128
    radices = radices_of(count)
    stages = len(radices)
    most = max(radices) - 1
    tiles = (2 * modes + 16) // 8 * lanes
    per = -(-tiles // count)
    f32 = jnp.float32
    block = jax.ShapeDtypeStruct((rows, width), jnp.bfloat16)
    state = jax.ShapeDtypeStruct((modes, width), f32)
    vmem = pl.BlockSpec(memory_space=pltpu.VMEM)
    dma = pltpu.SemaphoreType.DMA
    results = pl.pallas_call(
        functools.partial(kernel, count, tps, radices, per),
        out_shape=(
            block, block, block, block,
            jax.ShapeDtypeStruct((3, 3, width), f32), state, state,
            jax.ShapeDtypeStruct((1, width), f32), jax.ShapeDtypeStruct((8, 128), f32),
        ),
        in_specs=[vmem] * 8,
        out_specs=(vmem,) * 9,
        scratch_shapes=[
            pltpu.VMEM((2, 8, width), f32),
            pltpu.VMEM((2, 8, width), f32),
            pltpu.VMEM((3, rows + 16, width), f32),
            pltpu.VMEM((rows + 8, width), f32),
            pltpu.VMEM((3, rows + 8, width), f32),
            pltpu.VMEM((rows + 8, width), f32),
            pltpu.VMEM((rows + 8, width), f32),
            pltpu.VMEM((3, rows + 8, width), f32),
            pltpu.VMEM((rows, modes, width), f32),
            pltpu.VMEM((rows, modes, width), f32),
            pltpu.VMEM((lanes, rows * 8, 128), f32),
            pltpu.VMEM((lanes, rows * 8, 128), f32),
            pltpu.VMEM((stages, 2, modes, width), f32),
            pltpu.VMEM((stages, most, 2, modes, width), f32),
            pltpu.VMEM((count * per, 8, 128), f32),
            pltpu.VMEM((count, per, 8, 128), f32),
            pltpu.VMEM((count * per, 8, 128), f32),
            pltpu.VMEM((8, 128), f32),
            pltpu.VMEM((tps, 8, 128), f32),
            dma((2,)), dma((2,)), dma((stages, most)), dma((stages, most)),
            dma((count,)), dma((count,)), dma((count,)), dma((count,)), dma((tps,)), dma((tps,)),
        ],
        compiler_params=pltpu.CompilerParams(
            collective_id=0, has_side_effects=True, vmem_limit_bytes=40 * 1024 * 1024
        ),
        name="mixer",
    )(query_proj, key_proj, value_proj, out_grad, short_taps, residues, log_spans, skip_gain.reshape(1, width))
    mix, gq, gk, gv, gtaps, gres, glog, gskip, norm = results
    return mix, gq, gk, gv, gtaps, gres, glog, gskip.reshape(width), norm[0, 0]


def solution(mesh):
    whole, rows, cols = P("ctx", "tp"), P(None, "tp"), P(None, None, "tp")
    in_specs = (whole,) * 4 + (cols, rows, rows, P("tp"))
    out_specs = (whole,) * 4 + (cols, rows, rows, P("tp"), P())
    return jax.shard_map(body, mesh=mesh, in_specs=in_specs, out_specs=out_specs, check_vma=False)
```

time: 490 us -> 48.1 us (0.10); the launches traced: 480 us -> 47.7 us
  waiting for transfers between devices: 207 us -> 0 us
  blocking collectives: 96.5 us -> 0 us
  starting transfers between devices: 57.7 us -> 0 us
  matrix products: 41.3 us -> 0 us
  Pallas kernels: 0 us -> 35 us
  local copies, waits for them, and re-layouts: 44.5 us -> 12.1 us
  other arithmetic: 16.5 us -> 0 us
  between operations: 16.9 us -> 0.67 us
    psum x1 -> x0, waiting for transfers between devices: 102 us -> none  [body(): totals = lax.psum(packed, 'ctx')]
    all_to_all x12 -> x0, waiting for transfers between devices: 100 us -> none  [the longest x3 29.3 us: forward_seq(): lax.all_to_all(jnp.einsum('bks,sbc->bkc', joint_cos, pieces, precision=PR...]
    all_to_all x6 -> x0, blocking collectives: 93.4 us -> none  [the longest x2 35.1 us: inverse_seq(): lax.all_to_all(turned_imag, 'ctx', split_axis=0, concat_axis=1, tiled=True)]
    all_to_all x12 -> x0, starting transfers between devices: 51.5 us -> none  [the longest x3 12.5 us: forward_seq(): lax.all_to_all(jnp.einsum('bks,sbc->bkc', joint_sin, pieces, precision=PR...]
    dot_general x36 -> x0, matrix products: 41.3 us -> none  [the longest x6 8.75 us: dense_lead(): out_real = out_real - jnp.dot(sine, flat_imag, precision=PRECISE)]
    pallas_call x0 -> x1, Pallas kernels: none -> 35 us  [body(): pl.pallas_call(functools.partial(kernel, count, tps, radices, per), out_s...]
    all_to_all x18 -> x0, local copies, waits for them, and re-layouts: 20.8 us -> none  [the longest x6 8.55 us: inverse_seq(): lax.all_to_all(turned_imag, 'ctx', split_axis=0, concat_axis=1, tiled=True)]
    reshape x8 -> x0, local copies, waits for them, and re-layouts: 10.1 us -> none  [the longest x3 5.2 us: dense_lead(): out_real.reshape(real_part.shape)]
  transfers between devices with their start and end apart: 15 -> 0, of which waited for: 15 -> 0; matrix products, arithmetic and copies ran while one was open for 7% -> 0% of each run, Pallas kernels for 0% -> 0%
where the time goes in v1:
time: 48.1 us; the launch traced here: 47.7 us
  Pallas kernels  35 us (73%)
  local copies, waits for them, and re-layouts  12.1 us (25%)
  between operations  0.67 us (1%)
    pallas_call x1, Pallas kernels, body(): pl.pallas_call(functools.partial(kernel, count, tps, radices, per), out_s...  35 us
    unnamed x24, local copies, waits for them, and re-layouts  11.6 us

profile of v1, /device:TPU:0, one launch (start us, length us, event | category | flops | bytes accessed | tf_op | source)
XLA Modules:
  0.0 47.7 jit_solution(6634535228322484334)
XLA Ops:
  0.6 0.0 copy-start
  0.7 0.9 %copy-done = bf16[128,512]{1,0:T(8,128)(2,1)S(1)} copy-done((bf16[128,512]{1,0:T(8,128)(2,1)S(1)}, bf16[128,512]{1,0:T(8,128)(2,1)}, u32[]{:S(2)}) %copy-start) | copy-done | bytes 131096
  1.6 0.0 copy-start.1
  1.6 0.9 %copy-done.1 = bf16[128,512]{1,0:T(8,128)(2,1)S(1)} copy-done((bf16[128,512]{1,0:T(8,128)(2,1)S(1)}, bf16[128,512]{1,0:T(8,128)(2,1)}, u32[]{:S(2)}) %copy-start.1) | copy-done | bytes 131096
  2.5 0.0 copy-start.2
  2.5 0.9 %copy-done.2 = bf16[128,512]{1,0:T(8,128)(2,1)S(1)} copy-done((bf16[128,512]{1,0:T(8,128)(2,1)S(1)}, bf16[128,512]{1,0:T(8,128)(2,1)}, u32[]{:S(2)}) %copy-start.2) | copy-done | bytes 131096
  3.4 0.0 copy-start.3
  3.4 0.9 %copy-done.3 = bf16[128,512]{1,0:T(8,128)(2,1)S(1)} copy-done((bf16[128,512]{1,0:T(8,128)(2,1)S(1)}, bf16[128,512]{1,0:T(8,128)(2,1)}, u32[]{:S(2)}) %copy-start.3) | copy-done | bytes 131096
  4.3 0.0 copy-start.4
  4.3 0.8 %copy-done.4 = f32[16,512]{1,0:T(8,128)S(1)} copy-done((f32[16,512]{1,0:T(8,128)S(1)}, f32[16,512]{1,0:T(8,128)}, u32[]{:S(2)}) %copy-start.4) | copy-done | bytes 32792
  5.0 0.0 copy-start.5
  5.0 0.8 %copy-done.5 = f32[16,512]{1,0:T(8,128)S(1)} copy-done((f32[16,512]{1,0:T(8,128)S(1)}, f32[16,512]{1,0:T(8,128)}, u32[]{:S(2)}) %copy-start.5) | copy-done | bytes 32792
  5.8 0.0 copy-start.6
  5.8 0.7 %copy-done.6 = f32[3,3,512]{2,1,0:T(4,128)S(1)} copy-done((f32[3,3,512]{2,1,0:T(4,128)S(1)}, f32[3,3,512]{2,1,0:T(4,128)}, u32[]{:S(2)}) %copy-start.6) | copy-done | bytes 18456
  6.5 0.0 copy-start.7
  6.5 0.7 %copy-done.7 = f32[512]{0:T(512)S(1)} copy-done((f32[512]{0:T(512)S(1)}, f32[512]{0:T(512)}, u32[]{:S(2)}) %copy-start.7) | copy-done | bytes 2072
  7.2 35.0 %mixer.1 = (bf16[128,512]{1,0:T(8,128)(2,1)S(1)}, bf16[128,512]{1,0:T(8,128)(2,1)S(1)}, bf16[128,512]{1,0:T(8,128)(2,1)S(1)}, bf16[128,512]{1,0:T(8,128)(2,1)S(1...) custom-call(bf16[128,512]{1,0:T(8,128)(2,1)S(1)} %copy-done, ...), custom_call_target="tpu_custom_call" | custom-call | tf_op jit(solution)/shard_map/mixer/pallas_call | solution.py:395
  42.2 0.5 %slice.3 = f32[1,1]{1,0:T(1,128)} slice(f32[8,128]{1,0:T(8,128)S(1)} %get-tuple-element.26), slice={[0:1], [0:1]} | slice | bytes 8 | tf_op jit(solution)/shard_map/slice | solution.py:433
  42.7 0.7 %copy.25 = bf16[128,512]{1,0:T(8,128)(2,1)} copy(bf16[128,512]{1,0:T(8,128)(2,1)S(1)} %get-tuple-element.36) | data formatting | bytes 262144
  43.3 0.7 %copy.26 = bf16[128,512]{1,0:T(8,128)(2,1)} copy(bf16[128,512]{1,0:T(8,128)(2,1)S(1)} %get-tuple-element.37) | data formatting | bytes 262144
  44.0 0.7 %copy.27 = bf16[128,512]{1,0:T(8,128)(2,1)} copy(bf16[128,512]{1,0:T(8,128)(2,1)S(1)} %get-tuple-element.38) | data formatting | bytes 262144
  44.6 0.7 %copy.28 = bf16[128,512]{1,0:T(8,128)(2,1)} copy(bf16[128,512]{1,0:T(8,128)(2,1)S(1)} %get-tuple-element.39) | data formatting | bytes 262144
  45.3 0.6 %copy.29 = f32[3,3,512]{2,1,0:T(4,128)} copy(f32[3,3,512]{2,1,0:T(4,128)S(1)} %get-tuple-element.40) | data formatting | bytes 36864
  45.9 0.6 %copy.30 = f32[16,512]{1,0:T(8,128)} copy(f32[16,512]{1,0:T(8,128)S(1)} %get-tuple-element.41) | data formatting | bytes 65536
  46.5 0.6 %copy.31 = f32[16,512]{1,0:T(8,128)} copy(f32[16,512]{1,0:T(8,128)S(1)} %get-tuple-element.42) | data formatting | bytes 65536
  47.1 0.6 %copy.32 = f32[512]{0:T(512)} copy(f32[512]{0:T(512)S(1)} %bitcast.4) | data formatting | bytes 4096
Async XLA Ops:
  0.6 0.9 %copy-start = (bf16[128,512]{1,0:T(8,128)(2,1)S(1)}, bf16[128,512]{1,0:T(8,128)(2,1)}, u32[]{:S(2)}) copy-start(bf16[128,512]{1,0:T(8,128)(2,1)} %q_ref.1) | copy-start | bytes 393220
  1.6 0.9 %copy-start.1 = (bf16[128,512]{1,0:T(8,128)(2,1)S(1)}, bf16[128,512]{1,0:T(8,128)(2,1)}, u32[]{:S(2)}) copy-start(bf16[128,512]{1,0:T(8,128)(2,1)} %k_ref.1) | copy-start | bytes 393220
  2.5 0.9 %copy-start.2 = (bf16[128,512]{1,0:T(8,128)(2,1)S(1)}, bf16[128,512]{1,0:T(8,128)(2,1)}, u32[]{:S(2)}) copy-start(bf16[128,512]{1,0:T(8,128)(2,1)} %v_ref.1) | copy-start | bytes 393220
  3.4 0.9 %copy-start.3 = (bf16[128,512]{1,0:T(8,128)(2,1)S(1)}, bf16[128,512]{1,0:T(8,128)(2,1)}, u32[]{:S(2)}) copy-start(bf16[128,512]{1,0:T(8,128)(2,1)} %og_ref.1) | copy-start | bytes 393220
  4.3 0.8 %copy-start.4 = (f32[16,512]{1,0:T(8,128)S(1)}, f32[16,512]{1,0:T(8,128)}, u32[]{:S(2)}) copy-start(f32[16,512]{1,0:T(8,128)} %res_ref.1) | copy-start | bytes 98308
  5.0 0.8 %copy-start.5 = (f32[16,512]{1,0:T(8,128)S(1)}, f32[16,512]{1,0:T(8,128)}, u32[]{:S(2)}) copy-start(f32[16,512]{1,0:T(8,128)} %span_ref.1) | copy-start | bytes 98308
  5.8 0.7 %copy-start.6 = (f32[3,3,512]{2,1,0:T(4,128)S(1)}, f32[3,3,512]{2,1,0:T(4,128)}, u32[]{:S(2)}) copy-start(f32[3,3,512]{2,1,0:T(4,128)} %taps_ref.1) | copy-start | bytes 55300
  6.5 0.7 %copy-start.7 = (f32[512]{0:T(512)S(1)}, f32[512]{0:T(512)}, u32[]{:S(2)}) copy-start(f32[512]{0:T(512)} %param.15) | copy-start | bytes 6148

commit v2 on v1

--- a/solution.py
+++ b/solution.py
@@ -9,6 +9,7 @@
 
 MESH = pl.DeviceIdType.MESH
 UNROLL = 8
+VMEM_LIMIT = 62 * 1024 * 1024
 
 
 def radices_of(count):
@@ -22,8 +23,9 @@
 
 def kernel(
     count, tps, radices, per,
-    q_ref, k_ref, v_ref, og_ref, taps_ref, res_ref, span_ref, skip_ref,
+    q_hbm, k_hbm, v_hbm, og_hbm, taps_hbm, res_hbm, span_hbm, skip_hbm,
     mix_ref, gq_ref, gk_ref, gv_ref, gtaps_ref, gres_ref, glog_ref, gskip_ref, norm_ref,
+    q_ref, k_ref, v_ref, og_ref, taps_ref, res_ref, span_ref, skip_ref, load_sem,
     halo_out, halo_in, xe, og, sh, mx, ig, sg, hs, es, yp, zp,
     tot_out, tot_in, parts, parts_in, whole, norm_out, norm_in,
     halo_ss, halo_rs, tot_ss, tot_rs, part_ss, part_rs, whole_ss, whole_rs, norm_ss, norm_rs,
@@ -36,6 +38,12 @@
     lanes = width // 128
     ins = (q_ref, k_ref, v_ref)
 
+    froms = (q_hbm, k_hbm, v_hbm, og_hbm, taps_hbm, span_hbm, res_hbm, skip_hbm)
+    intos = (q_ref, k_ref, v_ref, og_ref, taps_ref, span_ref, res_ref, skip_ref)
+    loads = [pltpu.make_async_copy(a, b, load_sem.at[n]) for n, (a, b) in enumerate(zip(froms, intos))]
+    for load in loads:
+        load.start()
+
     def at(peer):
         return {"ctx": peer, "tp": core}
 
@@ -55,6 +63,8 @@
 
     lax.fori_loop(1, tps, greet_core, 0)
 
+    for load in loads[:4]:
+        load.wait()
     for w in range(3):
         xe[w, 0:8, :] = jnp.zeros((8, width), jnp.float32)
         xe[w, 8 : 8 + rows, :] = ins[w][...].astype(jnp.float32)
@@ -88,6 +98,8 @@
         mx[low : low + size, :] = sh[1, low : low + size, :] * sh[2, low : low + size, :]
         ig[low : low + size, :] = og[low : low + size, :] * sh[0, low : low + size, :]
 
+    for load in loads[4:]:
+        load.wait()
     short_rows(8, rows - 8)
     rates = jnp.exp(-span_ref[...])
     gains = jnp.sqrt(rates + 1.0 / length)
@@ -373,7 +385,16 @@
     squares = norm_in[0]
     for n in range(1, tps):
         squares = squares + norm_in[n]
-    norm_ref[...] = jnp.broadcast_to(jnp.sqrt(jnp.sum(squares, keepdims=True)), (8, 128))
+    norm_ref[...] = jnp.sqrt(jnp.sum(squares, keepdims=True))
+
+
+def write_out(*refs):
+    sem = refs[18]
+    copies = [pltpu.make_async_copy(refs[n], refs[9 + n], sem.at[n]) for n in range(9)]
+    for copy in copies:
+        copy.start()
+    for copy in copies:
+        copy.wait()
 
 
 def body(query_proj, key_proj, value_proj, out_grad, short_taps, residues, log_spans, skip_gain):
@@ -391,17 +412,25 @@
     block = jax.ShapeDtypeStruct((rows, width), jnp.bfloat16)
     state = jax.ShapeDtypeStruct((modes, width), f32)
     vmem = pl.BlockSpec(memory_space=pltpu.VMEM)
+    hbm = pl.BlockSpec(memory_space=pltpu.HBM)
     dma = pltpu.SemaphoreType.DMA
+    out_shape = (
+        block, block, block, block,
+        jax.ShapeDtypeStruct((3, 3, width), f32), state, state,
+        jax.ShapeDtypeStruct((1, width), f32), jax.ShapeDtypeStruct((1, 1), f32),
+    )
     results = pl.pallas_call(
         functools.partial(kernel, count, tps, radices, per),
-        out_shape=(
-            block, block, block, block,
-            jax.ShapeDtypeStruct((3, 3, width), f32), state, state,
-            jax.ShapeDtypeStruct((1, width), f32), jax.ShapeDtypeStruct((8, 128), f32),
-        ),
-        in_specs=[vmem] * 8,
+        out_shape=out_shape,
+        in_specs=[hbm] * 8,
         out_specs=(vmem,) * 9,
         scratch_shapes=[
+            *[pltpu.VMEM((rows, width), jnp.bfloat16)] * 4,
+            pltpu.VMEM((3, 3, width), f32),
+            pltpu.VMEM((modes, width), f32),
+            pltpu.VMEM((modes, width), f32),
+            pltpu.VMEM((1, width), f32),
+            dma((8,)),
             pltpu.VMEM((2, 8, width), f32),
             pltpu.VMEM((2, 8, width), f32),
             pltpu.VMEM((3, rows + 16, width), f32),
@@ -425,10 +454,19 @@
             dma((count,)), dma((count,)), dma((count,)), dma((count,)), dma((tps,)), dma((tps,)),
         ],
         compiler_params=pltpu.CompilerParams(
-            collective_id=0, has_side_effects=True, vmem_limit_bytes=40 * 1024 * 1024
+            collective_id=0, has_side_effects=True, vmem_limit_bytes=VMEM_LIMIT
         ),
         name="mixer",
     )(query_proj, key_proj, value_proj, out_grad, short_taps, residues, log_spans, skip_gain.reshape(1, width))
+    results = pl.pallas_call(
+        write_out,
+        out_shape=out_shape,
+        in_specs=[vmem] * 9,
+        out_specs=(hbm,) * 9,
+        scratch_shapes=[dma((9,))],
+        compiler_params=pltpu.CompilerParams(vmem_limit_bytes=VMEM_LIMIT),
+        name="write_out",
+    )(*results)
     mix, gq, gk, gv, gtaps, gres, glog, gskip, norm = results
     return mix, gq, gk, gv, gtaps, gres, glog, gskip.reshape(width), norm[0, 0]
 

time: 48.1 us -> 39.4 us (0.82)
  local copies, waits for them, and re-layouts: 12.1 us -> 0 us
  Pallas kernels: 35 us -> 38.6 us
    unnamed x24 -> x0, local copies, waits for them, and re-layouts: 11.6 us -> none
    pallas_call x0 -> x1, Pallas kernels: none -> 2.66 us  [body(): pl.pallas_call(write_out, out_shape=out_shape, in_specs=[vmem] * 9, out_s...]
    pallas_call x1, Pallas kernels: 35 us -> 35.9 us  [body(): pl.pallas_call(functools.partial(kernel, count, tps, radices, per), out_s...]
    slice x1 -> x0, local copies, waits for them, and re-layouts: 0.51 us -> none  [body(): norm[0, 0]]
where the time goes in v2:
time: 39.4 us; the launch traced here: 39.2 us
  Pallas kernels  38.6 us (98%)
  between operations  0.65 us (2%)
    pallas_call x1, Pallas kernels, body(): pl.pallas_call(functools.partial(kernel, count, tps, radices, per), out_s...  35.9 us
    pallas_call x1, Pallas kernels, body(): pl.pallas_call(write_out, out_shape=out_shape, in_specs=[vmem] * 9, out_s...  2.66 us

profile of v2, /device:TPU:0, one launch (start us, length us, event | category | flops | bytes accessed | tf_op | source)
XLA Modules:
  0.0 39.2 jit_solution(4493709520353169753)
XLA Ops:
  0.6 35.9 %mixer.1 = (bf16[128,512]{1,0:T(8,128)(2,1)}, bf16[128,512]{1,0:T(8,128)(2,1)}, bf16[128,512]{1,0:T(8,128)(2,1)}, bf16[128,512]{1,0:T(8,128)(2,1)}, f32[3,3,512]...) custom-call(bf16[128,512]{1,0:T(8,128)(2,1)} %q_hbm.1, ...), custom_call_target="tpu_custom_call" | custom-call | tf_op jit(solution)/shard_map/mixer/pallas_call | solution.py:422
  36.6 2.7 %write_out.1 = (bf16[128,512]{1,0:T(8,128)(2,1)}, bf16[128,512]{1,0:T(8,128)(2,1)}, bf16[128,512]{1,0:T(8,128)(2,1)}, bf16[128,512]{1,0:T(8,128)(2,1)}, f32[3,3,...) custom-call(bf16[128,512]{1,0:T(8,128)(2,1)} %get-tuple-element.27.refs_0_, ...), custom_call_target="tpu_custom_call" | custom-call | tf_op jit(solution)/shard_map/write_out/pallas_call | solution.py:461

commit v3 on v2

--- a/solution.py
+++ b/solution.py
@@ -24,8 +24,9 @@
 def kernel(
     count, tps, radices, per,
     q_hbm, k_hbm, v_hbm, og_hbm, taps_hbm, res_hbm, span_hbm, skip_hbm,
-    mix_ref, gq_ref, gk_ref, gv_ref, gtaps_ref, gres_ref, glog_ref, gskip_ref, norm_ref,
+    mix_hbm, gq_hbm, gk_hbm, gv_hbm, gtaps_hbm, gres_hbm, glog_hbm, gskip_hbm, norm_hbm,
     q_ref, k_ref, v_ref, og_ref, taps_ref, res_ref, span_ref, skip_ref, load_sem,
+    mix_ref, gq_ref, gk_ref, gv_ref, gtaps_ref, gres_ref, glog_ref, gskip_ref, norm_ref, store_sem,
     halo_out, halo_in, xe, og, sh, mx, ig, sg, hs, es, yp, zp,
     tot_out, tot_in, parts, parts_in, whole, norm_out, norm_in,
     halo_ss, halo_rs, tot_ss, tot_rs, part_ss, part_rs, whole_ss, whole_rs, norm_ss, norm_rs,
@@ -43,6 +44,10 @@
     loads = [pltpu.make_async_copy(a, b, load_sem.at[n]) for n, (a, b) in enumerate(zip(froms, intos))]
     for load in loads:
         load.start()
+
+    results = (mix_ref, gq_ref, gk_ref, gv_ref, gtaps_ref, gres_ref, glog_ref, gskip_ref, norm_ref)
+    places = (mix_hbm, gq_hbm, gk_hbm, gv_hbm, gtaps_hbm, gres_hbm, glog_hbm, gskip_hbm, norm_hbm)
+    stores = [pltpu.make_async_copy(a, b, store_sem.at[n]) for n, (a, b) in enumerate(zip(results, places))]
 
     def at(peer):
         return {"ctx": peer, "tp": core}
@@ -355,6 +360,8 @@
                 + taps_ref[w, 1:2, cols] * sg[w, 1 : rows + 1, cols]
                 + taps_ref[w, 2:3, cols] * sg[w, 2 : rows + 2, cols]
             ).astype(jnp.bfloat16)
+    for store in stores[:4]:
+        store.start()
     parts_in[me] = parts[pl.ds(me * per, per)]
     wait_all(part_copy, count)
 
@@ -381,11 +388,16 @@
             gtaps_ref[n // 3, n % 3 : n % 3 + 1, cols] = whole[(row // 8) * lanes + c, row % 8 : row % 8 + 1, :]
         row = 2 * modes + 9
         gskip_ref[:, cols] = whole[(row // 8) * lanes + c, row % 8 : row % 8 + 1, :]
+    for store in stores[4:8]:
+        store.start()
     wait_all(norm_copy, tps)
     squares = norm_in[0]
     for n in range(1, tps):
         squares = squares + norm_in[n]
     norm_ref[...] = jnp.sqrt(jnp.sum(squares, keepdims=True))
+    stores[8].start()
+    for store in stores:
+        store.wait()
 
 
 def write_out(*refs):
@@ -423,7 +435,7 @@
         functools.partial(kernel, count, tps, radices, per),
         out_shape=out_shape,
         in_specs=[hbm] * 8,
-        out_specs=(vmem,) * 9,
+        out_specs=(hbm,) * 9,
         scratch_shapes=[
             *[pltpu.VMEM((rows, width), jnp.bfloat16)] * 4,
             pltpu.VMEM((3, 3, width), f32),
@@ -431,6 +443,8 @@
             pltpu.VMEM((modes, width), f32),
             pltpu.VMEM((1, width), f32),
             dma((8,)),
+            *[pltpu.VMEM(item.shape, item.dtype) for item in out_shape],
+            dma((9,)),
             pltpu.VMEM((2, 8, width), f32),
             pltpu.VMEM((2, 8, width), f32),
             pltpu.VMEM((3, rows + 16, width), f32),

time: 39.4 us -> 39.3 us (level)
  no operation moved by 1% of the time
where the time goes in v3:
time: 39.3 us; the launch traced here: 39.2 us
  Pallas kernels  38.5 us (98%)
  between operations  0.65 us (2%)
    pallas_call x1, Pallas kernels, body(): pl.pallas_call(functools.partial(kernel, count, tps, radices, per), out_s...  35.8 us
    pallas_call x1, Pallas kernels, body(): pl.pallas_call(write_out, out_shape=out_shape, in_specs=[vmem] * 9, out_s...  2.66 us

profile of v3, /device:TPU:0, one launch (start us, length us, event | category | flops | bytes accessed | tf_op | source)
XLA Modules:
  0.0 39.2 jit_solution(9387446268706838240)
XLA Ops:
  0.6 35.8 %mixer.1 = (bf16[128,512]{1,0:T(8,128)(2,1)}, bf16[128,512]{1,0:T(8,128)(2,1)}, bf16[128,512]{1,0:T(8,128)(2,1)}, bf16[128,512]{1,0:T(8,128)(2,1)}, f32[3,3,512]...) custom-call(bf16[128,512]{1,0:T(8,128)(2,1)} %q_hbm.1, ...), custom_call_target="tpu_custom_call" | custom-call | tf_op jit(solution)/shard_map/mixer/pallas_call | solution.py:434
  36.5 2.7 %write_out.1 = (bf16[128,512]{1,0:T(8,128)(2,1)}, bf16[128,512]{1,0:T(8,128)(2,1)}, bf16[128,512]{1,0:T(8,128)(2,1)}, bf16[128,512]{1,0:T(8,128)(2,1)}, f32[3,3,...) custom-call(bf16[128,512]{1,0:T(8,128)(2,1)} %get-tuple-element.27.refs_0_, ...), custom_call_target="tpu_custom_call" | custom-call | tf_op jit(solution)/shard_map/write_out/pallas_call | solution.py:475
